TPU v7x, 512 devices: a whole 4x8x8 slice. The times are simulated.
512 devices in a mesh: seq: 32 (over x_hi, z, core), head: 16 (over y, x_lo).
Axes of the slice: x: 4 (x_hi: 2, x_lo: 2; x = x_hi * 2 + x_lo), y: 8, z: 8, core: 2. Of those that a mesh axis runs over, the one named last changes fastest.
Arguments:
- query: bfloat16 [32768, 2048], P(('seq', 'head')), may hold values from -6 to 6
- key: bfloat16 [32768, 2048], P(('seq', 'head')), may hold values from -6 to 6
- value: bfloat16 [32768, 2048], P(('seq', 'head')), may hold values from -6 to 6
- attn_out: bfloat16 [32768, 2048], P(('seq', 'head')), may hold values from -6 to 6
- grad_out: bfloat16 [32768, 2048], P(('seq', 'head')), may hold values from -96 to 96
- lse: float32 [16, 32768], P('head', 'seq'), may hold values from 7.5 to 9
- band: int32 [32, 5], replicated, may hold values from 0 to 1, as said below
Outputs:
- grad_query: bfloat16 [32768, 2048], P(('seq', 'head'))
- grad_key: bfloat16 [32768, 2048], P(('seq', 'head'))
- grad_value: bfloat16 [32768, 2048], P(('seq', 'head'))
Inputs may be any that keep to these rules, and one draw needn't show every extreme that they name: `band`: column 2 (the block itself) is always 1; entries whose key block lies outside the video are 0; some block lists all 5 key blocks.
All inputs are finite; a program needn't handle non-finite values.
Results may differ from a plain program's by a relative error of at most 0.0055.
Values may be sent and summed in bfloat16 or wider, within the bound.
A program may use at most 64 MiB of HBM per device.

v0:
```python
import math

import jax
import jax.numpy as jnp
from jax import lax
from jax.sharding import PartitionSpec as P

R = 2


def from_behind(value, axis, steps):
    count = lax.axis_size(axis)
    first, last = (max(0, -steps), min(count, count - steps))
    return lax.ppermute(value, axis, [(source, source + steps) for source in range(first, last)])


def pair_grads(query_blk, grad_blk, lse_row, delta_row, key_blk, value_blk):
    scale = 1.0 / math.sqrt(query_blk.shape[1])
    scores = jnp.dot(query_blk, key_blk.T, preferred_element_type=jnp.float32) * scale
    probs = jnp.exp(scores - lse_row[:, None])
    probs_low = probs.astype(jnp.bfloat16)
    grad_value = jnp.dot(probs_low.T, grad_blk, preferred_element_type=jnp.float32)
    grad_prob = jnp.dot(grad_blk, value_blk.T, preferred_element_type=jnp.float32)
    grad_score = (probs * (grad_prob - delta_row[:, None]) * scale).astype(jnp.bfloat16)
    grad_query = jnp.dot(grad_score, key_blk, preferred_element_type=jnp.float32)
    grad_key = jnp.dot(grad_score.T, query_blk, preferred_element_type=jnp.float32)
    return (grad_query, grad_key, grad_value)


def block_grads(operands):
    query_rows, grad_rows, lse_rows, delta_rows, key_rows, value_rows = operands
    pieces = [pair_grads(query_rows, grad_rows, lse_rows[0], delta_rows[0], key_rows, value_rows)]
    return tuple(
        (jnp.concatenate([piece[which] for piece in pieces], axis=1) for which in range(3))
    )


def per_device(query, key, value, attn_out, grad_out, lse, band):
    query_here, key_here, value_here, out_here, grad_here = (
        lax.all_to_all(query, "head", split_axis=1, concat_axis=0, tiled=True),
        lax.all_to_all(key, "head", split_axis=1, concat_axis=0, tiled=True),
        lax.all_to_all(value, "head", split_axis=1, concat_axis=0, tiled=True),
        lax.all_to_all(attn_out, "head", split_axis=1, concat_axis=0, tiled=True),
        lax.all_to_all(grad_out, "head", split_axis=1, concat_axis=0, tiled=True),
    )
    nheads = lse.shape[0]
    rows = query_here.shape[0]
    width = query_here.shape[1]
    head_size = width // nheads
    product = grad_here.astype(jnp.float32) * out_here.astype(jnp.float32)
    delta = jnp.sum(product.reshape(rows, nheads, head_size), axis=2).T
    here = lax.axis_index("seq")
    zeros = jnp.zeros((rows, width), jnp.float32)

    def nothing(operands):
        return (zeros, zeros, zeros)

    acc_query, acc_key, acc_value = block_grads(
        (query_here, grad_here, lse, delta, key_here, value_here)
    )
    for offset in range(-R, R + 1):
        if offset == 0:
            continue
        column = offset + R
        key_far, value_far = from_behind((key_here, value_here), "seq", -offset)
        listed = band[here, column] == 1
        part_query, part_key, part_value = lax.cond(
            listed, block_grads, nothing, (query_here, grad_here, lse, delta, key_far, value_far)
        )
        acc_query = acc_query + part_query
        back_key, back_value = from_behind(
            (part_key.astype(jnp.bfloat16), part_value.astype(jnp.bfloat16)), "seq", offset
        )
        acc_key = acc_key + back_key.astype(jnp.float32)
        acc_value = acc_value + back_value.astype(jnp.float32)
    results = (
        acc_query.astype(jnp.bfloat16),
        acc_key.astype(jnp.bfloat16),
        acc_value.astype(jnp.bfloat16),
    )
    return (
        lax.all_to_all(results[0], "head", split_axis=0, concat_axis=1, tiled=True),
        lax.all_to_all(results[1], "head", split_axis=0, concat_axis=1, tiled=True),
        lax.all_to_all(results[2], "head", split_axis=0, concat_axis=1, tiled=True),
    )


def solution(mesh):
    in_specs = (
        P(("seq", "head"), None),
        P(("seq", "head"), None),
        P(("seq", "head"), None),
        P(("seq", "head"), None),
        P(("seq", "head"), None),
        P("head", "seq"),
        P(),
    )
    out_specs = (P(("seq", "head"), None), P(("seq", "head"), None), P(("seq", "head"), None))
    return jax.shard_map(
        per_device, mesh=mesh, in_specs=in_specs, out_specs=out_specs, check_vma=False
    )
```

profile of v0, /device:TPU:4, one launch (start us, length us, event | category | flops | bytes accessed | tf_op | source)
XLA Modules:
  0.0 222.3 jit_solution(1541873588977267889)
XLA Ops:
  2.4 7.8 %all-to-all-start.1 = ((bf16[64,16,128]{2,0,1:T(8,128)(2,1)}), bf16[64,16,128]{2,0,1:T(8,128)(2,1)S(1)}, u32[]{:S(2)}, u32[]{:S(2)}) async-start(bf16[64,16,128]{2,0,1:T(8,128)(2,1)} %copy_bitcast_fusion.6), calls=%async_computation.1 | async-start | bytes 524288 | tf_op jit(solution)/shard_map/all_to_all | solution.py:41
  11.9 10.3 %all-to-all-done.1 = bf16[64,16,128]{2,0,1:T(8,128)(2,1)S(1)} async-done(((bf16[64,16,128]{2,0,1:T(8,128)(2,1)}), bf16[64,16,128]{2,0,1:T(8,128)(2,1)S(1)}, u32[]{:S(2)}, u32[]{:S(2)}) %all-to-all-start.1) | async-done | bytes 262176 | tf_op jit(solution)/shard_map/all_to_all | solution.py:41
  22.2 4.2 %all-to-all-start.3 = ((bf16[64,16,128]{2,0,1:T(8,128)(2,1)}), bf16[64,16,128]{2,0,1:T(8,128)(2,1)}, u32[]{:S(2)}, u32[]{:S(2)}) async-start(bf16[64,16,128]{2,0,1:T(8,128)(2,1)} %copy_bitcast_fusion.4), calls=%async_computation.3 | async-start | bytes 524288 | tf_op jit(solution)/shard_map/all_to_all | solution.py:42
  28.2 9.2 %all-to-all-done.3 = bf16[64,16,128]{2,0,1:T(8,128)(2,1)} async-done(((bf16[64,16,128]{2,0,1:T(8,128)(2,1)}), bf16[64,16,128]{2,0,1:T(8,128)(2,1)}, u32[]{:S(2)}, u32[]{:S(2)}) %all-to-all-start.3) | async-done | bytes 262176 | tf_op jit(solution)/shard_map/all_to_all | solution.py:42
  37.4 3.5 %all-to-all-start.4 = ((bf16[64,16,128]{2,0,1:T(8,128)(2,1)}), bf16[64,16,128]{2,0,1:T(8,128)(2,1)S(1)}, u32[]{:S(2)}, u32[]{:S(2)}) async-start(bf16[64,16,128]{2,0,1:T(8,128)(2,1)} %copy_bitcast_fusion.3), calls=%async_computation.4 | async-start | bytes 524288 | tf_op jit(solution)/shard_map/all_to_all | solution.py:43
  42.6 9.0 %all-to-all-done.4 = bf16[64,16,128]{2,0,1:T(8,128)(2,1)S(1)} async-done(((bf16[64,16,128]{2,0,1:T(8,128)(2,1)}), bf16[64,16,128]{2,0,1:T(8,128)(2,1)S(1)}, u32[]{:S(2)}, u32[]{:S(2)}) %all-to-all-start.4) | async-done | bytes 262176 | tf_op jit(solution)/shard_map/all_to_all | solution.py:43
  51.6 3.5 %all-to-all-start.2 = ((bf16[64,16,128]{2,0,1:T(8,128)(2,1)}), bf16[64,16,128]{2,0,1:T(8,128)(2,1)S(1)}, u32[]{:S(2)}, u32[]{:S(2)}) async-start(bf16[64,16,128]{2,0,1:T(8,128)(2,1)} %copy_bitcast_fusion.5), calls=%async_computation.2 | async-start | bytes 524288 | tf_op jit(solution)/shard_map/all_to_all | solution.py:44
  55.9 9.9 %all-to-all-done.2 = bf16[64,16,128]{2,0,1:T(8,128)(2,1)S(1)} async-done(((bf16[64,16,128]{2,0,1:T(8,128)(2,1)}), bf16[64,16,128]{2,0,1:T(8,128)(2,1)S(1)}, u32[]{:S(2)}, u32[]{:S(2)}) %all-to-all-start.2) | async-done | bytes 262176 | tf_op jit(solution)/shard_map/all_to_all | solution.py:44
  65.9 3.5 %all-to-all-start = ((bf16[64,16,128]{2,0,1:T(8,128)(2,1)}), bf16[64,16,128]{2,0,1:T(8,128)(2,1)S(1)}, u32[]{:S(2)}, u32[]{:S(2)}) async-start(bf16[64,16,128]{2,0,1:T(8,128)(2,1)} %copy_bitcast_fusion.7), calls=%async_computation | async-start | bytes 524288 | tf_op jit(solution)/shard_map/all_to_all | solution.py:40
  72.9 11.2 %collective-permute-start.7 = (bf16[1024,128]{1,0:T(8,128)(2,1)}, bf16[1024,128]{1,0:T(8,128)(2,1)}, u32[]{:S(2)}, u32[]{:S(2)}) collective-permute-start(bf16[1024,128]{1,0:T(8,128)(2,1)} %bitcast.16), channel_id=1, source_target_pairs={{32,0},{48,16},{64,32},{80,48},{96,64},{112,80},{128,96},{144,112}... | collective-permute-start | bytes 786440 | tf_op jit(solution)/shard_map/ppermute | solution.py:14
  86.1 2.4 %collective-permute-start.3 = (bf16[1024,128]{1,0:T(8,128)(2,1)}, bf16[1024,128]{1,0:T(8,128)(2,1)}, u32[]{:S(2)}, u32[]{:S(2)}) collective-permute-start(bf16[1024,128]{1,0:T(8,128)(2,1)} %bitcast.16), channel_id=1, source_target_pairs={{0,16},{16,32},{32,48},{48,64},{64,80},{80,96},{96,112},{112,128},... | collective-permute-start | bytes 786440 | tf_op jit(solution)/shard_map/ppermute | solution.py:14
  93.1 2.8 %multiply_convert_fusion.4 = bf16[1024,1024]{1,0:T(8,128)(2,1)S(1)} fusion(f32[1024,1024]{1,0:T(8,128)S(1)} %fusion.43, bf16[1024,128]{1,0:T(8,128)(2,1)S(1)} %bitcast.121, bf16[1024,128]{1,0:T(8,128)(2,1)} %bitcast.16, f32[1024]{0:T(1024)S(1)} %sub.103, f32[1024]{0:T(1024)S(1)} %bitcast.140), kind=kOutput, calls=%fused_computation.28 | convolution fusion | flops 274726912 | bytes 6823936 | tf_op jit(solution)/shard_map/dot_general | solution.py:23
  97.7 5.7 %collective-permute-start.6 = (bf16[1024,128]{1,0:T(8,128)(2,1)S(1)}, bf16[1024,128]{1,0:T(8,128)(2,1)S(1)}, u32[]{:S(2)}, u32[]{:S(2)}) collective-permute-start(bf16[1024,128]{1,0:T(8,128)(2,1)S(1)} %bitcast.135), channel_id=1, source_target_pairs={{32,0},{48,16},{64,32},{80,48},{96,64},{112,80},{128,96},{144,112}... | collective-permute-start | bytes 786440 | tf_op jit(solution)/shard_map/ppermute | solution.py:14
  103.6 2.6 %collective-permute-start.4 = (bf16[1024,128]{1,0:T(8,128)(2,1)S(1)}, bf16[1024,128]{1,0:T(8,128)(2,1)}, u32[]{:S(2)}, u32[]{:S(2)}) collective-permute-start(bf16[1024,128]{1,0:T(8,128)(2,1)S(1)} %bitcast.136), channel_id=1, source_target_pairs={{16,0},{32,16},{48,32},{64,48},{80,64},{96,80},{112,96},{128,112},... | collective-permute-start | bytes 786440 | tf_op jit(solution)/shard_map/ppermute | solution.py:14
  106.1 2.8 %collective-permute-done = bf16[1024,128]{1,0:T(8,128)(2,1)} collective-permute-done((bf16[1024,128]{1,0:T(8,128)(2,1)S(1)}, bf16[1024,128]{1,0:T(8,128)(2,1)}, u32[]{:S(2)}, u32[]{:S(2)}) %collective-permute-start) | collective-permute-done | bytes 262176 | tf_op jit(solution)/shard_map/ppermute | solution.py:14
  112.3 8.6 %conditional.4 = (f32[1024,128]{1,0:T(8,128)}, f32[1024,128]{1,0:T(8,128)S(1)}, f32[1024,128]{1,0:T(8,128)S(1)}) conditional(s32[]{:T(128)} %bitcast.18, () %tuple.40, (bf16[1024,128]{1,0:T(8,128)(2,1)S(1)}, bf16[1024,128]{1,0:T(8,128)(2,1)}, f32[1,1024]{1,0:T(1,128)S(1)}, bf16[1024,128]{1,0:T(8,128)(2,1)S(1)}, bf16[1024,128]{1,0:T(8,128)(2,1)}, ...), branch_computations={%region_1.0_spmd, %region_2.0_spmd} | conditional | flops 1351614464 | bytes 22294552 | solution.py:67
  115.1 2.6 %multiply_convert_fusion = bf16[1024,1024]{1,0:T(8,128)(2,1)S(1)} fusion(f32[1024,1024]{1,0:T(8,128)S(1)} %fusion.31, bf16[1024,128]{1,0:T(8,128)(2,1)S(1)} %get-tuple-element.51, bf16[1024,128]{1,0:T(8,128)(2,1)} %get-tuple-element.52, f32[1024]{0:T(1024)S(1)} %bitcast.150, f32[1024]{0:T(1024)S(1)} %bitcast.143), kind=kOutput, calls=%fused_computation | convolution fusion | flops 274726912 | bytes 6823936 | tf_op jit(solution)/shard_map/cond/branch_1_fun/dot_general | solution.py:23
  118.4 2.5 %fusion.32 = f32[1024,128]{1,0:T(8,128)} fusion(bf16[1024,1024]{1,0:T(8,128)(2,1)S(1)} %multiply_convert_fusion, bf16[1024,128]{1,0:T(8,128)(2,1)} %get-tuple-element.49), kind=kOutput, calls=%fused_computation.53 | convolution fusion | flops 268435456 | bytes 2883584 | tf_op jit(solution)/shard_map/cond/branch_1_fun/dot_general | solution.py:25
  124.8 7.3 %collective-permute-start.13 = (bf16[1024,128]{1,0:T(8,128)(2,1)}, bf16[1024,128]{1,0:T(8,128)(2,1)}, u32[]{:S(2)}, u32[]{:S(2)}) collective-permute-start(bf16[1024,128]{1,0:T(8,128)(2,1)} %convert_element_type.149), channel_id=1, source_target_pairs={{16,0},{32,16},{48,32},{64,48},{80,64},{96,80},{112,96},{128,112},... | collective-permute-start | bytes 786440 | tf_op jit(solution)/shard_map/ppermute | solution.py:14
  135.2 6.6 %conditional.7 = (f32[1024,128]{1,0:T(8,128)S(1)}, f32[1024,128]{1,0:T(8,128)S(1)}, f32[1024,128]{1,0:T(8,128)S(1)}) conditional(s32[]{:T(128)} %bitcast.25, () %tuple.46, (bf16[1024,128]{1,0:T(8,128)(2,1)S(1)}, bf16[1024,128]{1,0:T(8,128)(2,1)S(1)}, f32[1,1024]{1,0:T(1,128)S(1)}, bf16[1024,128]{1,0:T(8,128)(2,1)S(1)}, bf16[1024,128]{1,0:T(8,128)(2,1)}, ...), branch_computations={%region_7.0_spmd, %region_8.0_spmd} | conditional | flops 1351614464 | bytes 24391760 | solution.py:67
  137.7 2.6 %multiply_convert_fusion.3 = bf16[1024,1024]{1,0:T(8,128)(2,1)S(1)} fusion(f32[1024,1024]{1,0:T(8,128)S(1)} %fusion.40, bf16[1024,128]{1,0:T(8,128)(2,1)S(1)} %get-tuple-element.69, bf16[1024,128]{1,0:T(8,128)(2,1)} %get-tuple-element.70, f32[1024]{0:T(1024)S(1)} %bitcast.153, f32[1024]{0:T(1024)S(1)} %bitcast.149), kind=kOutput, calls=%fused_computation.21 | convolution fusion | flops 274726912 | bytes 6823936 | tf_op jit(solution)/shard_map/cond/branch_1_fun/dot_general | solution.py:23
  142.6 11.2 %collective-permute-start.15 = (bf16[1024,128]{1,0:T(8,128)(2,1)}, bf16[1024,128]{1,0:T(8,128)(2,1)}, u32[]{:S(2)}, u32[]{:S(2)}) collective-permute-start(bf16[1024,128]{1,0:T(8,128)(2,1)} %convert_element_type.153), channel_id=1, source_target_pairs={{0,32},{16,48},{32,64},{48,80},{64,96},{80,112},{96,128},{112,144}... | collective-permute-start | bytes 786440 | tf_op jit(solution)/shard_map/ppermute | solution.py:14
  153.8 2.5 %add_convert_fusion.2 = bf16[1024,128]{1,0:T(8,128)(2,1)} fusion(f32[1024,128]{1,0:T(8,128)S(1)} %get-tuple-element.90, f32[1024,128]{1,0:T(8,128)} %copy-done.11, f32[1024,128]{1,0:T(8,128)} %copy-done.10, f32[1024,128]{1,0:T(8,128)} %fusion.44, f32[1024,128]{1,0:T(8,128)} %get-tuple-element.87), kind=kLoop, calls=%fused_computation.38 | loop fusion | flops 655360 | bytes 2883584 | tf_op jit(solution)/shard_map/convert_element_type | solution.py:77
  156.3 8.7 %all-to-all-start.5 = ((bf16[16,64,128]{2,1,0:T(8,128)(2,1)}), bf16[16,64,128]{2,1,0:T(8,128)(2,1)}, u32[]{:S(2)}, u32[]{:S(2)}) async-start(bf16[16,64,128]{2,1,0:T(8,128)(2,1)} %bitcast.139), calls=%async_computation.5 | async-start | bytes 524288 | tf_op jit(solution)/shard_map/all_to_all | solution.py:82
  165.0 3.3 %fusion.25 = f32[1024,128]{1,0:T(8,128)S(1)} fusion(bf16[1024,128]{1,0:T(8,128)(2,1)S(1)} %bitcast.126, f32[1024,1024]{1,0:T(8,128)} %copy-done.1, f32[1024]{0:T(1024)S(1)} %bitcast.141), kind=kOutput, calls=%fused_computation.31 | convolution fusion | flops 271581184 | bytes 4984832 | tf_op jit(solution)/shard_map/dot_general | solution.py:22
  172.5 6.1 %collective-permute-start.9 = (bf16[1024,128]{1,0:T(8,128)(2,1)}, bf16[1024,128]{1,0:T(8,128)(2,1)}, u32[]{:S(2)}, u32[]{:S(2)}) collective-permute-start(bf16[1024,128]{1,0:T(8,128)(2,1)} %convert_element_type.139), channel_id=1, source_target_pairs={{16,0},{32,16},{48,32},{64,48},{80,64},{96,80},{112,96},{128,112},... | collective-permute-start | bytes 786440 | tf_op jit(solution)/shard_map/ppermute | solution.py:14
  180.7 3.5 %collective-permute-start.11 = (bf16[1024,128]{1,0:T(8,128)(2,1)S(1)}, bf16[1024,128]{1,0:T(8,128)(2,1)}, u32[]{:S(2)}, u32[]{:S(2)}) collective-permute-start(bf16[1024,128]{1,0:T(8,128)(2,1)S(1)} %convert_element_type.143), channel_id=1, source_target_pairs={{0,32},{16,48},{32,64},{48,80},{64,96},{80,112},{96,128},{112,144}... | collective-permute-start | bytes 786440 | tf_op jit(solution)/shard_map/ppermute | solution.py:14
  184.2 2.1 add_convert_fusion
  186.3 8.4 %all-to-all-start.7 = ((bf16[16,64,128]{2,1,0:T(8,128)(2,1)}), bf16[16,64,128]{2,1,0:T(8,128)(2,1)S(1)}, u32[]{:S(2)}, u32[]{:S(2)}) async-start(bf16[16,64,128]{2,1,0:T(8,128)(2,1)} %bitcast.30), calls=%async_computation.7 | async-start | bytes 524288 | tf_op jit(solution)/shard_map/all_to_all | solution.py:84
  199.0 8.0 %all-to-all-done.7 = bf16[16,64,128]{2,1,0:T(8,128)(2,1)S(1)} async-done(((bf16[16,64,128]{2,1,0:T(8,128)(2,1)}), bf16[16,64,128]{2,1,0:T(8,128)(2,1)S(1)}, u32[]{:S(2)}, u32[]{:S(2)}) %all-to-all-start.7) | async-done | bytes 262176 | tf_op jit(solution)/shard_map/all_to_all | solution.py:84
  206.9 3.5 %all-to-all-start.6 = ((bf16[16,64,128]{2,1,0:T(8,128)(2,1)}), bf16[16,64,128]{2,1,0:T(8,128)(2,1)S(1)}, u32[]{:S(2)}, u32[]{:S(2)}) async-start(bf16[16,64,128]{2,1,0:T(8,128)(2,1)} %bitcast.28), calls=%async_computation.6 | async-start | bytes 524288 | tf_op jit(solution)/shard_map/all_to_all | solution.py:83
  212.9 8.6 %all-to-all-done.6 = bf16[16,64,128]{2,1,0:T(8,128)(2,1)S(1)} async-done(((bf16[16,64,128]{2,1,0:T(8,128)(2,1)}), bf16[16,64,128]{2,1,0:T(8,128)(2,1)S(1)}, u32[]{:S(2)}, u32[]{:S(2)}) %all-to-all-start.6) | async-done | bytes 262176 | tf_op jit(solution)/shard_map/all_to_all | solution.py:83
  (98 shorter events, 49.4 us)
Async XLA Ops:
  0.6 54.5 %copy-start.15 = (bf16[64,2048]{1,0:T(8,128)(2,1)S(1)}, bf16[64,2048]{1,0:T(8,128)(2,1)}, u32[]{:S(2)}) copy-start(bf16[64,2048]{1,0:T(8,128)(2,1)} %param.15) | copy-start | bytes 786436
  0.7 68.8 %copy-start.16 = (s32[32,5]{0,1:T(8,128)S(1)}, s32[32,5]{0,1:T(8,128)}, u32[]{:S(2)}) copy-start(s32[32,5]{0,1:T(8,128)} %param.21) | copy-start | bytes 1924
  2.4 19.9 %all-to-all-start.1 = ((bf16[64,16,128]{2,0,1:T(8,128)(2,1)}), bf16[64,16,128]{2,0,1:T(8,128)(2,1)S(1)}, u32[]{:S(2)}, u32[]{:S(2)}) async-start(bf16[64,16,128]{2,0,1:T(8,128)(2,1)} %copy_bitcast_fusion.6), calls=%async_computation.1 | async-start | bytes 524288 | tf_op jit(solution)/shard_map/all_to_all | solution.py:41
  22.2 15.1 %all-to-all-start.3 = ((bf16[64,16,128]{2,0,1:T(8,128)(2,1)}), bf16[64,16,128]{2,0,1:T(8,128)(2,1)}, u32[]{:S(2)}, u32[]{:S(2)}) async-start(bf16[64,16,128]{2,0,1:T(8,128)(2,1)} %copy_bitcast_fusion.4), calls=%async_computation.3 | async-start | bytes 524288 | tf_op jit(solution)/shard_map/all_to_all | solution.py:42
  26.4 66.6 %copy-start.14 = (f32[1,1024]{1,0:T(1,128)S(1)}, f32[1,1024]{1,0:T(1,128)}, u32[]{:S(2)}) copy-start(f32[1,1024]{1,0:T(1,128)} %param.20) | copy-start | bytes 12292
  37.4 14.3 %all-to-all-start.4 = ((bf16[64,16,128]{2,0,1:T(8,128)(2,1)}), bf16[64,16,128]{2,0,1:T(8,128)(2,1)S(1)}, u32[]{:S(2)}, u32[]{:S(2)}) async-start(bf16[64,16,128]{2,0,1:T(8,128)(2,1)} %copy_bitcast_fusion.3), calls=%async_computation.4 | async-start | bytes 524288 | tf_op jit(solution)/shard_map/all_to_all | solution.py:43
  51.6 14.3 %all-to-all-start.2 = ((bf16[64,16,128]{2,0,1:T(8,128)(2,1)}), bf16[64,16,128]{2,0,1:T(8,128)(2,1)S(1)}, u32[]{:S(2)}, u32[]{:S(2)}) async-start(bf16[64,16,128]{2,0,1:T(8,128)(2,1)} %copy_bitcast_fusion.5), calls=%async_computation.2 | async-start | bytes 524288 | tf_op jit(solution)/shard_map/all_to_all | solution.py:44
  65.9 26.5 %all-to-all-start = ((bf16[64,16,128]{2,0,1:T(8,128)(2,1)}), bf16[64,16,128]{2,0,1:T(8,128)(2,1)S(1)}, u32[]{:S(2)}, u32[]{:S(2)}) async-start(bf16[64,16,128]{2,0,1:T(8,128)(2,1)} %copy_bitcast_fusion.7), calls=%async_computation | async-start | bytes 524288 | tf_op jit(solution)/shard_map/all_to_all | solution.py:40
  72.9 62.2 %collective-permute-start.7 = (bf16[1024,128]{1,0:T(8,128)(2,1)}, bf16[1024,128]{1,0:T(8,128)(2,1)}, u32[]{:S(2)}, u32[]{:S(2)}) collective-permute-start(bf16[1024,128]{1,0:T(8,128)(2,1)} %bitcast.16), channel_id=1, source_target_pairs={{32,0},{48,16},{64,32},{80,48},{96,64},{112,80},{128,96},{144,112}... | collective-permute-start | bytes 786440 | tf_op jit(solution)/shard_map/ppermute | solution.py:14
  84.1 40.7 %collective-permute-start.5 = (bf16[1024,128]{1,0:T(8,128)(2,1)}, bf16[1024,128]{1,0:T(8,128)(2,1)}, u32[]{:S(2)}, u32[]{:S(2)}) collective-permute-start(bf16[1024,128]{1,0:T(8,128)(2,1)} %bitcast.16), channel_id=1, source_target_pairs={{16,0},{32,16},{48,32},{64,48},{80,64},{96,80},{112,96},{128,112},... | collective-permute-start | bytes 786440 | tf_op jit(solution)/shard_map/ppermute | solution.py:14
  86.1 11.6 %collective-permute-start.3 = (bf16[1024,128]{1,0:T(8,128)(2,1)}, bf16[1024,128]{1,0:T(8,128)(2,1)}, u32[]{:S(2)}, u32[]{:S(2)}) collective-permute-start(bf16[1024,128]{1,0:T(8,128)(2,1)} %bitcast.16), channel_id=1, source_target_pairs={{0,16},{16,32},{32,48},{48,64},{64,80},{80,96},{96,112},{112,128},... | collective-permute-start | bytes 786440 | tf_op jit(solution)/shard_map/ppermute | solution.py:14
  88.5 15.1 %collective-permute-start.1 = (bf16[1024,128]{1,0:T(8,128)(2,1)}, bf16[1024,128]{1,0:T(8,128)(2,1)}, u32[]{:S(2)}, u32[]{:S(2)}) collective-permute-start(bf16[1024,128]{1,0:T(8,128)(2,1)} %bitcast.16), channel_id=1, source_target_pairs={{0,32},{16,48},{32,64},{48,80},{64,96},{80,112},{96,128},{112,144}... | collective-permute-start | bytes 786440 | tf_op jit(solution)/shard_map/ppermute | solution.py:14
  90.4 18.5 %collective-permute-start = (bf16[1024,128]{1,0:T(8,128)(2,1)S(1)}, bf16[1024,128]{1,0:T(8,128)(2,1)}, u32[]{:S(2)}, u32[]{:S(2)}) collective-permute-start(bf16[1024,128]{1,0:T(8,128)(2,1)S(1)} %bitcast.133), channel_id=1, source_target_pairs={{0,32},{16,48},{32,64},{48,80},{64,96},{80,112},{96,128},{112,144}... | collective-permute-start | bytes 786440 | tf_op jit(solution)/shard_map/ppermute | solution.py:14
  93.1 19.3 %copy-start.1 = (f32[1024,1024]{1,0:T(8,128)}, f32[1024,1024]{1,0:T(8,128)S(1)}, u32[]{:S(2)}) copy-start(f32[1024,1024]{1,0:T(8,128)S(1)} %fusion.43) | copy-start | bytes 12582916
  97.7 37.5 %collective-permute-start.6 = (bf16[1024,128]{1,0:T(8,128)(2,1)S(1)}, bf16[1024,128]{1,0:T(8,128)(2,1)S(1)}, u32[]{:S(2)}, u32[]{:S(2)}) collective-permute-start(bf16[1024,128]{1,0:T(8,128)(2,1)S(1)} %bitcast.135), channel_id=1, source_target_pairs={{32,0},{48,16},{64,32},{80,48},{96,64},{112,80},{128,96},{144,112}... | collective-permute-start | bytes 786440 | tf_op jit(solution)/shard_map/ppermute | solution.py:14
  103.6 28.6 %collective-permute-start.4 = (bf16[1024,128]{1,0:T(8,128)(2,1)S(1)}, bf16[1024,128]{1,0:T(8,128)(2,1)}, u32[]{:S(2)}, u32[]{:S(2)}) collective-permute-start(bf16[1024,128]{1,0:T(8,128)(2,1)S(1)} %bitcast.136), channel_id=1, source_target_pairs={{16,0},{32,16},{48,32},{64,48},{80,64},{96,80},{112,96},{128,112},... | collective-permute-start | bytes 786440 | tf_op jit(solution)/shard_map/ppermute | solution.py:14
  108.9 12.8 %collective-permute-start.2 = (bf16[1024,128]{1,0:T(8,128)(2,1)S(1)}, bf16[1024,128]{1,0:T(8,128)(2,1)}, u32[]{:S(2)}, u32[]{:S(2)}) collective-permute-start(bf16[1024,128]{1,0:T(8,128)(2,1)S(1)} %bitcast.137), channel_id=1, source_target_pairs={{0,16},{16,32},{32,48},{48,64},{64,80},{80,96},{96,112},{112,128},... | collective-permute-start | bytes 786440 | tf_op jit(solution)/shard_map/ppermute | solution.py:14
  121.7 50.8 %collective-permute-start.12 = (bf16[1024,128]{1,0:T(8,128)(2,1)}, bf16[1024,128]{1,0:T(8,128)(2,1)}, u32[]{:S(2)}, u32[]{:S(2)}) collective-permute-start(bf16[1024,128]{1,0:T(8,128)(2,1)} %convert_element_type.147), channel_id=1, source_target_pairs={{32,0},{48,16},{64,32},{80,48},{96,64},{112,80},{128,96},{144,112}... | collective-permute-start | bytes 786440 | tf_op jit(solution)/shard_map/ppermute | solution.py:14
  124.0 8.1 %copy-start.4 = (f32[1024,128]{1,0:T(8,128)}, f32[1024,128]{1,0:T(8,128)S(1)}, u32[]{:S(2)}) copy-start(f32[1024,128]{1,0:T(8,128)S(1)} %get-tuple-element.92) | copy-start | bytes 1572868
  124.0 8.1 %copy-start.10 = (f32[1024,128]{1,0:T(8,128)}, f32[1024,128]{1,0:T(8,128)S(1)}, u32[]{:S(2)}) copy-start(f32[1024,128]{1,0:T(8,128)S(1)} %get-tuple-element.88) | copy-start | bytes 1572868
  124.8 53.8 %collective-permute-start.13 = (bf16[1024,128]{1,0:T(8,128)(2,1)}, bf16[1024,128]{1,0:T(8,128)(2,1)}, u32[]{:S(2)}, u32[]{:S(2)}) collective-permute-start(bf16[1024,128]{1,0:T(8,128)(2,1)} %convert_element_type.149), channel_id=1, source_target_pairs={{16,0},{32,16},{48,32},{64,48},{80,64},{96,80},{112,96},{128,112},... | collective-permute-start | bytes 786440 | tf_op jit(solution)/shard_map/ppermute | solution.py:14
  133.1 47.5 %collective-permute-start.14 = (bf16[1024,128]{1,0:T(8,128)(2,1)}, bf16[1024,128]{1,0:T(8,128)(2,1)}, u32[]{:S(2)}, u32[]{:S(2)}) collective-permute-start(bf16[1024,128]{1,0:T(8,128)(2,1)} %convert_element_type.151), channel_id=1, source_target_pairs={{0,16},{16,32},{32,48},{48,64},{64,80},{80,96},{96,112},{112,128},... | collective-permute-start | bytes 786440 | tf_op jit(solution)/shard_map/ppermute | solution.py:14
  141.8 12.0 %copy-start.8 = (f32[1024,128]{1,0:T(8,128)}, f32[1024,128]{1,0:T(8,128)S(1)}, u32[]{:S(2)}) copy-start(f32[1024,128]{1,0:T(8,128)S(1)} %get-tuple-element.94) | copy-start | bytes 1572868
  142.6 41.6 %collective-permute-start.15 = (bf16[1024,128]{1,0:T(8,128)(2,1)}, bf16[1024,128]{1,0:T(8,128)(2,1)}, u32[]{:S(2)}, u32[]{:S(2)}) collective-permute-start(bf16[1024,128]{1,0:T(8,128)(2,1)} %convert_element_type.153), channel_id=1, source_target_pairs={{0,32},{16,48},{32,64},{48,80},{64,96},{80,112},{96,128},{112,144}... | collective-permute-start | bytes 786440 | tf_op jit(solution)/shard_map/ppermute | solution.py:14
  153.8 14.5 %copy-start.3 = (f32[1024,128]{1,0:T(8,128)S(1)}, f32[1024,128]{1,0:T(8,128)}, u32[]{:S(2)}) copy-start(f32[1024,128]{1,0:T(8,128)} %copy-done.2) | copy-start | bytes 1572868
  156.3 30.0 %all-to-all-start.5 = ((bf16[16,64,128]{2,1,0:T(8,128)(2,1)}), bf16[16,64,128]{2,1,0:T(8,128)(2,1)}, u32[]{:S(2)}, u32[]{:S(2)}) async-start(bf16[16,64,128]{2,1,0:T(8,128)(2,1)} %bitcast.139), calls=%async_computation.5 | async-start | bytes 524288 | tf_op jit(solution)/shard_map/all_to_all | solution.py:82
  169.1 26.3 %collective-permute-start.8 = (bf16[1024,128]{1,0:T(8,128)(2,1)}, bf16[1024,128]{1,0:T(8,128)(2,1)S(1)}, u32[]{:S(2)}, u32[]{:S(2)}) collective-permute-start(bf16[1024,128]{1,0:T(8,128)(2,1)} %convert_element_type.137), channel_id=1, source_target_pairs={{32,0},{48,16},{64,32},{80,48},{96,64},{112,80},{128,96},{144,112}... | collective-permute-start | bytes 786440 | tf_op jit(solution)/shard_map/ppermute | solution.py:14
  172.5 22.9 %collective-permute-start.9 = (bf16[1024,128]{1,0:T(8,128)(2,1)}, bf16[1024,128]{1,0:T(8,128)(2,1)}, u32[]{:S(2)}, u32[]{:S(2)}) collective-permute-start(bf16[1024,128]{1,0:T(8,128)(2,1)} %convert_element_type.139), channel_id=1, source_target_pairs={{16,0},{32,16},{48,32},{64,48},{80,64},{96,80},{112,96},{128,112},... | collective-permute-start | bytes 786440 | tf_op jit(solution)/shard_map/ppermute | solution.py:14
  178.6 16.8 %collective-permute-start.10 = (bf16[1024,128]{1,0:T(8,128)(2,1)}, bf16[1024,128]{1,0:T(8,128)(2,1)}, u32[]{:S(2)}, u32[]{:S(2)}) collective-permute-start(bf16[1024,128]{1,0:T(8,128)(2,1)} %convert_element_type.141), channel_id=1, source_target_pairs={{0,16},{16,32},{32,48},{48,64},{64,80},{80,96},{96,112},{112,128},... | collective-permute-start | bytes 786440 | tf_op jit(solution)/shard_map/ppermute | solution.py:14
  180.7 16.4 %collective-permute-start.11 = (bf16[1024,128]{1,0:T(8,128)(2,1)S(1)}, bf16[1024,128]{1,0:T(8,128)(2,1)}, u32[]{:S(2)}, u32[]{:S(2)}) collective-permute-start(bf16[1024,128]{1,0:T(8,128)(2,1)S(1)} %convert_element_type.143), channel_id=1, source_target_pairs={{0,32},{16,48},{32,64},{48,80},{64,96},{80,112},{96,128},{112,144}... | collective-permute-start | bytes 786440 | tf_op jit(solution)/shard_map/ppermute | solution.py:14
  186.3 20.7 %all-to-all-start.7 = ((bf16[16,64,128]{2,1,0:T(8,128)(2,1)}), bf16[16,64,128]{2,1,0:T(8,128)(2,1)S(1)}, u32[]{:S(2)}, u32[]{:S(2)}) async-start(bf16[16,64,128]{2,1,0:T(8,128)(2,1)} %bitcast.30), calls=%async_computation.7 | async-start | bytes 524288 | tf_op jit(solution)/shard_map/all_to_all | solution.py:84
  206.9 14.6 %all-to-all-start.6 = ((bf16[16,64,128]{2,1,0:T(8,128)(2,1)}), bf16[16,64,128]{2,1,0:T(8,128)(2,1)S(1)}, u32[]{:S(2)}, u32[]{:S(2)}) async-start(bf16[16,64,128]{2,1,0:T(8,128)(2,1)} %bitcast.28), calls=%async_computation.6 | async-start | bytes 524288 | tf_op jit(solution)/shard_map/all_to_all | solution.py:83
  (9 other events, 33.7 us)
where the time goes:
time: 224 us; the launch traced here: 222 us
  starting transfers between devices  109 us (49%)
  waiting for transfers between devices  61.4 us (27%)
  matrix products  23.5 us (10%)
  local copies, waits for them, and re-layouts  12.6 us (6%)
  other arithmetic  12.1 us (5%)
  between operations  3.73 us (2%)
    ppermute x16, starting transfers between devices, from_behind(): lax.ppermute(value, axis, [(source, source + steps) for source in range(f...  65.5 us
    all_to_all x1, waiting for transfers between devices, per_device(): lax.all_to_all(key, 'head', split_axis=1, concat_axis=0, tiled=True)  10.3 us
    all_to_all x1, waiting for transfers between devices, per_device(): lax.all_to_all(grad_out, 'head', split_axis=1, concat_axis=0, tiled=True)  9.93 us
    all_to_all x1, waiting for transfers between devices, per_device(): lax.all_to_all(value, 'head', split_axis=1, concat_axis=0, tiled=True)  9.17 us
    all_to_all x1, waiting for transfers between devices, per_device(): lax.all_to_all(attn_out, 'head', split_axis=1, concat_axis=0, tiled=True)  8.99 us
    all_to_all x1, starting transfers between devices, per_device(): lax.all_to_all(results[0], 'head', split_axis=0, concat_axis=1, tiled=True)  8.7 us
    all_to_all x1, waiting for transfers between devices, per_device(): lax.all_to_all(results[1], 'head', split_axis=0, concat_axis=1, tiled=True)  8.63 us
    all_to_all x1, starting transfers between devices, per_device(): lax.all_to_all(results[2], 'head', split_axis=0, concat_axis=1, tiled=True)  8.38 us
  transfers between devices with their start and end apart: 24, of which 10 were waited for; matrix products, arithmetic and copies ran while one was open for 20% of the time, Pallas kernels for 0%

commit v1 on v0

v1 whole, which is shorter than its diff:
```python
import math

import jax
import jax.numpy as jnp
from jax import lax
from jax.experimental import pallas as pl
from jax.experimental.pallas import tpu as pltpu
from jax.sharding import PartitionSpec as P

R = 2
HD = 128
SLOTS = 2 * R
LOG2E = 1.4426950408889634
SCALE = 1.0 / math.sqrt(HD)
UNLISTED = 1e30
MESH = pl.DeviceIdType.MESH
NT = (((1,), (1,)), ((), ()))
NN = (((1,), (0,)), ((), ()))


def dot(a, b, dims):
    return lax.dot_general(a, b, dims, preferred_element_type=jnp.float32)


def slot_step(slot, sign):
    return sign * (1 + slot // 2) * (1 - 2 * ((slot * (3 - slot)) // 2))


def far_slot(slot):
    return jnp.where(slot < 2, slot, 5 - slot)


def kernel(
    nseq,
    nhead,
    query,
    key,
    value,
    attn_out,
    grad_out,
    lse,
    band,
    out_query,
    out_key,
    out_value,
    own_qg,
    own_kv,
    far_qg,
    own_rows,
    far_rows,
    delta_out,
    delta_in,
    key_t,
    acc_query,
    acc_key,
    acc_value,
    term_out,
    term_in,
    res_query,
    res_kv,
    qg_send,
    qg_recv,
    kv_send,
    kv_recv,
    delta_send,
    delta_recv,
    far_send,
    far_recv,
    rows_send,
    rows_recv,
    term_send,
    term_recv,
    res_send,
    res_recv,
):
    here = lax.axis_index("seq")
    head = lax.axis_index("head")
    sign = 1 - 2 * lax.rem(here, 2)
    rows = query.shape[0]
    block = rows * nhead

    def cols(which):
        return pl.ds(pl.multiple_of(which * HD, HD), HD)

    def part(which):
        return pl.ds(pl.multiple_of(which * rows, rows), rows)

    def peer(step):
        return lax.rem(head + step, nhead)

    def neighbour(slot):
        other = here + slot_step(slot, sign)
        return other, jnp.logical_and(other >= 0, other < nseq)

    def remote(src, dst, send, recv, **where):
        return pltpu.make_async_remote_copy(
            src_ref=src, dst_ref=dst, send_sem=send, recv_sem=recv,
            device_id=where, device_id_type=MESH,
        )

    def drain(ref, sem):
        pltpu.make_async_copy(ref, ref, sem).wait()

    barrier = pltpu.get_barrier_semaphore()

    def greet(step, carry):
        pl.semaphore_signal(barrier, inc=1, device_id={"head": peer(step)}, device_id_type=MESH)
        return carry

    lax.fori_loop(1, nhead, greet, 0)
    for slot in range(SLOTS):
        other, inside = neighbour(slot)

        @pl.when(inside)
        def _(other=other):
            pl.semaphore_signal(barrier, inc=1, device_id={"seq": other}, device_id_type=MESH)

    count = nhead - 1
    for slot in range(SLOTS):
        count = count + jnp.where(neighbour(slot)[1], 1, 0)
    pl.semaphore_wait(barrier, count)

    def send_qg(step, carry):
        to = peer(step)
        remote(query.at[:, cols(to)], own_qg.at[0, part(head), :], qg_send, qg_recv, head=to).start()
        remote(grad_out.at[:, cols(to)], own_qg.at[1, part(head), :], qg_send, qg_recv, head=to).start()
        return carry

    lax.fori_loop(1, nhead, send_qg, 0)
    pltpu.make_async_copy(query.at[:, cols(head)], own_qg.at[0, part(head), :], qg_recv).start()
    pltpu.make_async_copy(grad_out.at[:, cols(head)], own_qg.at[1, part(head), :], qg_recv).start()

    lane = lax.broadcasted_iota(jnp.int32, (rows, HD), 1)
    sums = jnp.zeros((rows, HD), jnp.float32)
    for which in range(nhead):
        at = slice(which * HD, (which + 1) * HD)
        product = grad_out[:, at].astype(jnp.float32) * attn_out[:, at].astype(jnp.float32)
        sums = jnp.where(lane == which, jnp.sum(product, axis=1, keepdims=True), sums)
    across = jnp.concatenate([sums, sums], axis=0).T
    half = lax.broadcasted_iota(jnp.int32, (1, HD), 1) // rows
    across = jnp.where(half == lax.rem(head, 2), across, 0.0)
    for which in range(nhead):
        delta_out[which] = across[which : which + 1, :]

    def send_delta(step, carry):
        to = peer(step)
        remote(delta_out.at[to], delta_in.at[head], delta_send, delta_recv, head=to).start()
        return carry

    lax.fori_loop(1, nhead, send_delta, 0)
    pltpu.make_async_copy(delta_out.at[head], delta_in.at[head], delta_recv).start()

    def send_kv(step, carry):
        to = peer(step)
        remote(key.at[:, cols(to)], own_kv.at[0, part(head), :], kv_send, kv_recv, head=to).start()
        remote(value.at[:, cols(to)], own_kv.at[1, part(head), :], kv_send, kv_recv, head=to).start()
        return carry

    lax.fori_loop(1, nhead, send_kv, 0)
    pltpu.make_async_copy(key.at[:, cols(head)], own_kv.at[0, part(head), :], kv_recv).start()
    pltpu.make_async_copy(value.at[:, cols(head)], own_kv.at[1, part(head), :], kv_recv).start()

    drain(delta_in, delta_recv)
    own_rows[0:1, :] = lse[...] * LOG2E + math.log2(1.0 / SCALE)
    for pair in range(block // HD):
        own_rows[1:2, pair * HD : (pair + 1) * HD] = delta_in[2 * pair] + delta_in[2 * pair + 1]
    drain(own_qg, qg_recv)

    for slot in range(SLOTS):
        other, inside = neighbour(slot)

        @pl.when(inside)
        def _(slot=slot, other=other):
            there = slot if slot < 2 else 5 - slot
            remote(own_qg, far_qg.at[there], far_send.at[slot], far_recv.at[there], seq=other).start()
            remote(own_rows, far_rows.at[there], rows_send.at[slot], rows_recv.at[there], seq=other).start()

    acc_query[...] = jnp.zeros_like(acc_query)
    acc_key[...] = jnp.zeros_like(acc_key)
    acc_value[...] = jnp.zeros_like(acc_value)
    drain(own_kv, kv_recv)
    key_t[...] = own_kv[0].T
    chunk = min(256, block)

    def pair_grads(qg, shift, delta):
        def step(index, carry):
            at = pl.ds(pl.multiple_of(index * chunk, chunk), chunk)
            query_rows = qg[0]
            grad_rows = qg[1]
            scores = dot(own_kv[0, at, :], query_rows, NT)
            probs = jnp.exp2(scores * (SCALE * LOG2E) - shift)
            grad_prob = dot(own_kv[1, at, :], grad_rows, NT)
            probs_low = probs.astype(jnp.bfloat16)
            grad_score = (probs * (grad_prob - delta)).astype(jnp.bfloat16)
            acc_value[at, :] += dot(probs_low, grad_rows, NN)
            acc_key[at, :] += dot(grad_score, query_rows, NN)
            acc_query[...] += dot(key_t[:, at], grad_score, NN)
            return carry

        lax.fori_loop(0, block // chunk, step, 0)

    def far_pair(slot, carry):
        other, inside = neighbour(slot)

        @pl.when(inside)
        def _():
            there = far_slot(slot)
            drain(far_rows.at[slot], rows_recv.at[slot])
            drain(far_qg.at[slot], far_recv.at[slot])
            listed = band[other, here - other + R] == 1
            shift = jnp.where(listed, far_rows[slot, 0:1, :], UNLISTED)
            pair_grads(far_qg.at[slot], shift, far_rows[slot, 1:2, :])
            term_out[slot] = acc_query[...].astype(jnp.bfloat16)
            acc_query[...] = jnp.zeros_like(acc_query)
            remote(term_out.at[slot], term_in.at[there], term_send.at[slot], term_recv.at[there], seq=other).start()

        return carry

    lax.fori_loop(0, SLOTS, far_pair, 0)
    pair_grads(own_qg, own_rows[0:1, :], own_rows[1:2, :])

    def send_result(src, out, which):
        def step(index, carry):
            to = peer(index)
            remote(src.at[part(to), :], out.at[:, cols(head)], res_send.at[which], res_recv.at[which], head=to).start()
            return carry

        lax.fori_loop(1, nhead, step, 0)
        pltpu.make_async_copy(src.at[part(head), :], out.at[:, cols(head)], res_recv.at[which]).start()

    res_kv[0] = acc_key[...].astype(jnp.bfloat16)
    send_result(res_kv.at[0], out_key, 1)
    res_kv[1] = (acc_value[...] * (1.0 / SCALE)).astype(jnp.bfloat16)
    send_result(res_kv.at[1], out_value, 2)

    for slot in range(SLOTS):
        other, inside = neighbour(slot)

        @pl.when(inside)
        def _(slot=slot):
            drain(term_in.at[slot], term_recv.at[slot])
            acc_query[...] += term_in[slot].astype(jnp.float32)

    res_query[...] = acc_query[...].T.astype(jnp.bfloat16)
    send_result(res_query, out_query, 0)

    sent = pl.ds(0, (nhead - 1) * rows)
    drain(own_qg.at[:, sent, :], qg_send)
    drain(own_kv.at[:, sent, :], kv_send)
    drain(delta_in.at[pl.ds(0, nhead - 1)], delta_send)
    for slot in range(SLOTS):

        @pl.when(neighbour(slot)[1])
        def _(slot=slot):
            drain(own_qg, far_send.at[slot])
            drain(own_rows, rows_send.at[slot])
            drain(term_out.at[slot], term_send.at[slot])

    for which in range(3):
        drain(res_query.at[sent, :], res_send.at[which])
    drain(out_key, res_recv.at[1])
    drain(out_value, res_recv.at[2])
    drain(out_query, res_recv.at[0])


def per_device(query, key, value, attn_out, grad_out, lse, band):
    nseq, nhead = lax.axis_size("seq"), lax.axis_size("head")
    rows, width = query.shape
    block = rows * nhead
    low, full = jnp.bfloat16, jnp.float32
    vmem = pl.BlockSpec(memory_space=pltpu.VMEM)
    result = jax.ShapeDtypeStruct((rows, width), low)
    dma = pltpu.SemaphoreType.DMA

    def body(*refs):
        kernel(nseq, nhead, *refs)

    return pl.pallas_call(
        body,
        out_shape=(result,) * 3,
        in_specs=[vmem] * 6 + [pl.BlockSpec(memory_space=pltpu.SMEM)],
        out_specs=[vmem] * 3,
        scratch_shapes=[
            pltpu.VMEM((2, block, HD), low),
            pltpu.VMEM((2, block, HD), low),
            pltpu.VMEM((SLOTS, 2, block, HD), low),
            pltpu.VMEM((2, block), full),
            pltpu.VMEM((SLOTS, 2, block), full),
            pltpu.VMEM((nhead, 1, HD), full),
            pltpu.VMEM((nhead, 1, HD), full),
            pltpu.VMEM((HD, block), low),
            pltpu.VMEM((HD, block), full),
            pltpu.VMEM((block, HD), full),
            pltpu.VMEM((block, HD), full),
            pltpu.VMEM((SLOTS, HD, block), low),
            pltpu.VMEM((SLOTS, HD, block), low),
            pltpu.VMEM((block, HD), low),
            pltpu.VMEM((2, block, HD), low),
            dma, dma, dma, dma, dma, dma,
            dma((SLOTS,)), dma((SLOTS,)),
            dma((SLOTS,)), dma((SLOTS,)),
            dma((SLOTS,)), dma((SLOTS,)),
            dma((3,)), dma((3,)),
        ],
        compiler_params=pltpu.CompilerParams(
            collective_id=0, has_side_effects=True, vmem_limit_bytes=48 * 2**20
        ),
        cost_estimate=pl.CostEstimate(
            flops=25 * 2 * block * block * HD, bytes_accessed=8 * rows * width * 2,
            transcendentals=5 * block * block,
        ),
        name="attention_grads",
    )(query, key, value, attn_out, grad_out, lse, band)


def solution(mesh):
    rows = P(("seq", "head"), None)
    return jax.shard_map(
        per_device, mesh=mesh, in_specs=(rows,) * 5 + (P("head", "seq"), P()),
        out_specs=(rows,) * 3, check_vma=False,
    )
```

time: 224 us -> 85.9 us (0.38)
  the two profiles are of different devices: /device:TPU:4 before, /device:TPU:20 now
where the time goes in v1:
time: 85.9 us; the launch traced here: 85.6 us
  Pallas kernels  77.3 us (90%)
  local copies, waits for them, and re-layouts  7.64 us (9%)
    pallas_call x1, Pallas kernels, per_device(): pl.pallas_call(body, out_shape=(result,) * 3, in_specs=[vmem] * 6 + [pl.B...  77.3 us
    unnamed x16, local copies, waits for them, and re-layouts  7.64 us

profile of v1, /device:TPU:20, one launch (start us, length us, event | category | flops | bytes accessed | tf_op | source)
XLA Modules:
  0.0 85.6 jit_solution(17931687235458904583)
XLA Ops:
  0.6 0.0 copy-start.5
  0.6 0.8 copy.10.refs_6_
  1.4 0.0 copy-done.5
  1.4 0.0 copy-start
  1.4 0.9 %copy-done = bf16[64,2048]{1,0:T(8,128)(2,1)S(1)} copy-done((bf16[64,2048]{1,0:T(8,128)(2,1)S(1)}, bf16[64,2048]{1,0:T(8,128)(2,1)}, u32[]{:S(2)}) %copy-start) | copy-done | bytes 262168
  2.4 0.0 copy-start.1
  2.4 0.9 %copy-done.1 = bf16[64,2048]{1,0:T(8,128)(2,1)S(1)} copy-done((bf16[64,2048]{1,0:T(8,128)(2,1)S(1)}, bf16[64,2048]{1,0:T(8,128)(2,1)}, u32[]{:S(2)}) %copy-start.1) | copy-done | bytes 262168
  3.3 0.0 copy-start.2
  3.3 0.9 %copy-done.2 = bf16[64,2048]{1,0:T(8,128)(2,1)S(1)} copy-done((bf16[64,2048]{1,0:T(8,128)(2,1)S(1)}, bf16[64,2048]{1,0:T(8,128)(2,1)}, u32[]{:S(2)}) %copy-start.2) | copy-done | bytes 262168
  4.3 0.0 copy-start.3
  4.3 0.9 %copy-done.3 = bf16[64,2048]{1,0:T(8,128)(2,1)S(1)} copy-done((bf16[64,2048]{1,0:T(8,128)(2,1)S(1)}, bf16[64,2048]{1,0:T(8,128)(2,1)}, u32[]{:S(2)}) %copy-start.3) | copy-done | bytes 262168
  5.2 0.0 copy-start.4
  5.2 0.9 %copy-done.4 = bf16[64,2048]{1,0:T(8,128)(2,1)S(1)} copy-done((bf16[64,2048]{1,0:T(8,128)(2,1)S(1)}, bf16[64,2048]{1,0:T(8,128)(2,1)}, u32[]{:S(2)}) %copy-start.4) | copy-done | bytes 262168
  6.2 77.3 %attention_grads.1 = (bf16[64,2048]{1,0:T(8,128)(2,1)S(1)}, bf16[64,2048]{1,0:T(8,128)(2,1)S(1)}, bf16[64,2048]{1,0:T(8,128)(2,1)S(1)}) custom-call(bf16[64,2048]{1,0:T(8,128)(2,1)S(1)} %copy-done, bf16[64,2048]{1,0:T(8,128)(2,1)S(1)} %copy-done.1, bf16[64,2048]{1,0:T(8,128)(2,1)S(1)} %copy-done.2, bf16[64,2048]{1,0:T(8,128)(2,1)S(1)} %copy-done.3, ...), custom_call_target="tpu_custom_call" | custom-call | flops 6710886400 | bytes 2097152 | tf_op jit(solution)/shard_map/attention_grads/pallas_call | solution.py:278
  83.5 0.7 copy.14
  84.2 0.7 copy.15
  84.9 0.7 copy.16
Async XLA Ops:
  0.6 0.8 copy-start.5
  1.4 1.0 %copy-start = (bf16[64,2048]{1,0:T(8,128)(2,1)S(1)}, bf16[64,2048]{1,0:T(8,128)(2,1)}, u32[]{:S(2)}) copy-start(bf16[64,2048]{1,0:T(8,128)(2,1)} %refs_0_.1) | copy-start | bytes 786436
  2.4 0.9 %copy-start.1 = (bf16[64,2048]{1,0:T(8,128)(2,1)S(1)}, bf16[64,2048]{1,0:T(8,128)(2,1)}, u32[]{:S(2)}) copy-start(bf16[64,2048]{1,0:T(8,128)(2,1)} %refs_1_.1) | copy-start | bytes 786436
  3.3 0.9 %copy-start.2 = (bf16[64,2048]{1,0:T(8,128)(2,1)S(1)}, bf16[64,2048]{1,0:T(8,128)(2,1)}, u32[]{:S(2)}) copy-start(bf16[64,2048]{1,0:T(8,128)(2,1)} %refs_2_.1) | copy-start | bytes 786436
  4.3 0.9 %copy-start.3 = (bf16[64,2048]{1,0:T(8,128)(2,1)S(1)}, bf16[64,2048]{1,0:T(8,128)(2,1)}, u32[]{:S(2)}) copy-start(bf16[64,2048]{1,0:T(8,128)(2,1)} %refs_3_.1) | copy-start | bytes 786436
  5.2 0.9 %copy-start.4 = (bf16[64,2048]{1,0:T(8,128)(2,1)S(1)}, bf16[64,2048]{1,0:T(8,128)(2,1)}, u32[]{:S(2)}) copy-start(bf16[64,2048]{1,0:T(8,128)(2,1)} %refs_4_.1) | copy-start | bytes 786436

commit v2 on v1

v2 whole, which is shorter than its diff:
```python
import math

import jax
import jax.numpy as jnp
from jax import lax
from jax.experimental import pallas as pl
from jax.experimental.pallas import tpu as pltpu
from jax.sharding import PartitionSpec as P

R = 2
HD = 128
SLOTS = 2 * R
OWN = SLOTS
PARTS = 4
FIRST = 4
AFTER = ((1, (4,)), (2, (5,)), (3, (6,)))
NEAR = 1
LOG2E = 1.4426950408889634
SCALE = 1.0 / math.sqrt(HD)
UNLISTED = 1e30
MESH = pl.DeviceIdType.MESH
NT = (((1,), (1,)), ((), ()))
NN = (((1,), (0,)), ((), ()))


def dot(a, b, dims):
    return lax.dot_general(a, b, dims, preferred_element_type=jnp.float32)


def slot_step(slot, sign):
    return sign * (1 + slot // 2) * (1 - 2 * ((slot * (3 - slot)) // 2))


def far_slot(slot):
    return jnp.where(slot < 2, slot, 5 - slot)


def kernel(
    nseq,
    nhead,
    query_hbm,
    key_hbm,
    value_hbm,
    attn_out_hbm,
    grad_out_hbm,
    lse_hbm,
    band,
    out_query,
    out_key,
    out_value,
    query,
    key,
    value,
    attn_out,
    grad_out,
    lse,
    lse_rows,
    across,
    qg,
    kv,
    rows_of,
    delta_out,
    delta_in,
    key_t,
    acc_query,
    acc_part,
    acc_key,
    acc_value,
    term_out,
    term_in,
    res_query,
    res_kv,
    load_sem,
    qg_send,
    qg_recv,
    kv_send,
    kv_recv,
    delta_send,
    delta_recv,
    far_send,
    far_recv,
    rows_send,
    rows_recv,
    term_send,
    term_recv,
    res_send,
    res_recv,
    ready,
):
    here = lax.axis_index("seq")
    head = lax.axis_index("head")
    sign = 1 - 2 * lax.rem(here, 2)
    row = nseq // 2 if nseq >= 8 * R else nseq
    place_in_row = lax.rem(here, row)
    rows = query.shape[0]
    block = rows * nhead
    chunk = block // PARTS
    per = nhead // PARTS
    ny = nhead // 2

    def cols(which):
        return pl.ds(pl.multiple_of(which * HD, HD), HD)

    def part(which):
        return pl.ds(pl.multiple_of(which * rows, rows), rows)

    def quarter(which):
        return pl.ds(pl.multiple_of(which * chunk, chunk), chunk)

    def offset(place):
        if ny != 8:
            return place // 2, place % 2
        group, which = place // 4, place % 4
        reach = jnp.where(group == 3, 2, 1 + 2 * (which // 2))
        along_y = jnp.where(which % 2 == 1, ny - reach, reach)
        along_y = jnp.where(group == 0, 4 * (which // 2), along_y)
        along_x = jnp.where(group == 0, which % 2, jnp.where(group == 3, which // 2, group - 1))
        return along_y, along_x

    def sender(place):
        along_y, along_x = offset(place)
        return 2 * lax.rem(head // 2 + ny - along_y, ny) + lax.rem(head + along_x, 2)

    def receiver(place):
        along_y, along_x = offset(place)
        return 2 * lax.rem(head // 2 + along_y, ny) + lax.rem(head + along_x, 2)

    def after(step):
        return lax.rem(head + step, nhead)

    def neighbour(slot):
        other = here + slot_step(slot, sign)
        return other, jnp.logical_and(other >= 0, other < nseq)

    def standing(slot):
        other, inside = neighbour(slot)
        ahead = lax.rem(other + nseq, row) - place_in_row
        later = jnp.logical_and(inside, ahead > 0)
        earlier = jnp.logical_and(inside, ahead < 0)
        return other, later, earlier, jnp.logical_and(inside, ahead > R)

    def ordered(turn):
        last = jnp.where(turn < 3, lax.rem(turn + 1, 3), turn)
        slot = jnp.where(place_in_row == 0, lax.rem(SLOTS - turn, SLOTS), turn)
        slot = jnp.where(place_in_row == row - 1, last, slot)
        return jnp.where(place_in_row == row - 2, lax.rem(turn + 3, SLOTS), slot)

    def remote(src, dst, send, recv, **where):
        return pltpu.make_async_remote_copy(
            src_ref=src, dst_ref=dst, send_sem=send, recv_sem=recv,
            device_id=where, device_id_type=MESH,
        )

    def drain(ref, sem):
        pltpu.make_async_copy(ref, ref, sem).wait()

    loads = [
        pltpu.make_async_copy(src, dst, load_sem.at[at])
        for at, (src, dst) in enumerate(
            (
                (query_hbm, query),
                (grad_out_hbm, grad_out),
                (attn_out_hbm, attn_out),
                (key_hbm, key),
                (value_hbm, value),
                (lse_hbm, lse),
            )
        )
    ]
    for load in loads:
        load.start()

    barrier = pltpu.get_barrier_semaphore()

    def greet(step, carry):
        pl.semaphore_signal(barrier, inc=1, device_id={"head": after(step)}, device_id_type=MESH)
        return carry

    lax.fori_loop(1, nhead, greet, 0)
    count = nhead - 1
    for slot in range(SLOTS):
        other, later, earlier, _ = standing(slot)
        count = count + jnp.where(earlier, 1, 0)

        @pl.when(later)
        def _(other=other):
            pl.semaphore_signal(barrier, inc=1, device_id={"seq": other}, device_id_type=MESH)

    pl.semaphore_wait(barrier, count)
    for slot in range(SLOTS):
        other, _, earlier, _ = standing(slot)

        @pl.when(earlier)
        def _(slot=slot, other=other):
            there = slot if slot < 2 else 5 - slot
            pl.semaphore_signal(ready.at[there], inc=1, device_id={"seq": other}, device_id_type=MESH)

    def exchange(first, second, dst, send, recv, index):
        def step(place, carry):
            to = receiver(place)

            @pl.when(place > 0)
            def _():
                remote(first.at[:, cols(to)], dst.at[0, part(place), :], send, recv.at[index], head=to).start()
                remote(second.at[:, cols(to)], dst.at[1, part(place), :], send, recv.at[index], head=to).start()

            return carry

        lax.fori_loop(index * per, index * per + per, step, 0)

    def packet(number):
        if number < PARTS:
            exchange(query, grad_out, qg.at[OWN], qg_send, qg_recv, number)
        else:
            exchange(key, value, kv, kv_send, kv_recv, number - PARTS)

    for load in loads[:2] + loads[3:5]:
        load.wait()
    for number in range(FIRST):
        packet(number)
    for at, (first, second) in enumerate(((query, grad_out), (key, value))):
        dst, recv = ((qg.at[OWN], qg_recv), (kv, kv_recv))[at]
        pltpu.make_async_copy(first.at[:, cols(head)], dst.at[0, part(0), :], recv.at[0]).start()
        pltpu.make_async_copy(second.at[:, cols(head)], dst.at[1, part(0), :], recv.at[0]).start()

    loads[2].wait()
    lane = lax.broadcasted_iota(jnp.int32, (rows, HD), 1)
    sums = jnp.zeros((rows, HD), jnp.float32)
    for which in range(nhead):
        at = slice(which * HD, (which + 1) * HD)
        product = grad_out[:, at].astype(jnp.float32) * attn_out[:, at].astype(jnp.float32)
        sums = jnp.where(lane == which, jnp.sum(product, axis=1, keepdims=True), sums)
    across[...] = jnp.concatenate([sums, sums], axis=0).T
    low_half = lax.broadcasted_iota(jnp.int32, (1, HD), 1) < rows
    for place in range(nhead):
        to = receiver(place)
        mine = low_half if place % 2 == 0 else jnp.logical_not(low_half)
        delta_out[place] = jnp.where(mine, across[pl.ds(to, 1), :], 0.0)
        if place:
            remote(delta_out.at[place], delta_in.at[place], delta_send, delta_recv, head=to).start()
        else:
            pltpu.make_async_copy(delta_out.at[0], delta_in.at[0], delta_recv).start()

    loads[5].wait()
    lanes = block // HD
    for at in range(lanes):
        lse_rows[at : at + 1, :] = lse[:, at * HD : (at + 1) * HD]

    def lse_half(place):
        source = sender(place)
        one = lse_rows[pl.ds(source // 2, 1), :]
        other = jnp.concatenate([one[:, rows:], one[:, :rows]], axis=1)
        return jnp.where(lax.rem(source, 2) == place % 2, one, other)

    for at in range(lanes):
        turned = jnp.where(low_half, lse_half(2 * at), lse_half(2 * at + 1))
        rows_of[OWN, 0:1, at * HD : (at + 1) * HD] = turned * LOG2E + math.log2(1.0 / SCALE)
    acc_query[...] = jnp.zeros_like(acc_query)
    acc_key[...] = jnp.zeros_like(acc_key)
    acc_value[...] = jnp.zeros_like(acc_value)

    def forward_piece(slot, index, other):
        there = slot if slot < 2 else 5 - slot
        at = quarter(index)
        remote(
            qg.at[OWN, :, at, :], qg.at[there, :, at, :],
            far_send.at[slot, index], far_recv.at[there, index], seq=other,
        ).start()

    def forward(index, carry):
        drain(qg.at[OWN, :, quarter(index), :], qg_recv.at[index])
        for slot in range(SLOTS):
            other, later, earlier, late = standing(slot)
            prompt = jnp.logical_and(later, jnp.logical_not(late))
            @pl.when(prompt)
            def _(slot=slot, other=other):
                @pl.when(index == 0)
                def _():
                    pl.semaphore_wait(ready.at[slot], 1)

                if slot != 2:
                    forward_piece(slot, index, other)

            @pl.when(jnp.logical_and(earlier, slot != 2))
            def _(slot=slot, other=other):
                forward_piece(slot, index, other)

        for moment, numbers in AFTER:

            @pl.when(index == moment)
            def _(numbers=numbers):
                for number in numbers:
                    packet(number)

        return carry

    lax.fori_loop(0, PARTS, forward, 0)

    passing = neighbour(1)[1]
    behind = jnp.logical_and(passing, place_in_row == 0)

    def pass_on(index, carry):
        at = quarter(index)
        drain(qg.at[1, :, at, :], far_recv.at[1, index])
        remote(
            qg.at[1, :, at, :], qg.at[3, :, at, :],
            far_send.at[2, index], far_recv.at[3, index], seq=neighbour(0)[0],
        ).start()
        return carry

    drain(delta_in, delta_recv)
    for at in range(lanes):
        rows_of[OWN, 1:2, at * HD : (at + 1) * HD] = delta_in[2 * at] + delta_in[2 * at + 1]
    for slot in range(SLOTS):
        other, inside = neighbour(slot)

        @pl.when(standing(slot)[3])
        def _(slot=slot, other=other):
            pl.semaphore_wait(ready.at[slot], 1)
            if slot != 2:
                for index in range(PARTS):
                    forward_piece(slot, index, other)

        @pl.when(inside)
        def _(slot=slot, other=other):
            there = slot if slot < 2 else 5 - slot
            remote(rows_of.at[OWN], rows_of.at[there], rows_send.at[slot], rows_recv.at[there], seq=other).start()

    @pl.when(jnp.logical_and(passing, jnp.logical_not(behind)))
    def _():
        lax.fori_loop(0, PARTS, pass_on, 0)

    def arrive(index):
        at = quarter(index)
        drain(kv.at[:, at, :], kv_recv.at[index])

        @pl.when(index == 0)
        def _():
            for number in range(AFTER[-1][1][-1] + 1, 2 * PARTS):
                packet(number)

        key_t[index] = kv[0, at, :].T

    def item(index, slot):
        at = quarter(index)
        query_rows = qg[slot, 0]
        grad_rows = qg[slot, 1]
        scores = dot(kv[0, at, :], query_rows, NT)
        probs = jnp.exp2(scores * (SCALE * LOG2E) - rows_of[slot, 0:1, :])
        grad_prob = dot(kv[1, at, :], grad_rows, NT)
        probs_low = probs.astype(jnp.bfloat16)
        grad_score = (probs * (grad_prob - rows_of[slot, 1:2, :])).astype(jnp.bfloat16)
        acc_value[at, :] += dot(probs_low, grad_rows, NN)
        acc_key[at, :] += dot(grad_score, query_rows, NN)
        acc_query[slot] += dot(key_t[index], grad_score, NN)

    def far_item(index, slot):
        other, inside = neighbour(slot)

        @pl.when(inside)
        def _():
            @pl.when(index == 0)
            def _():
                drain(rows_of.at[slot], rows_recv.at[slot])
                listed = band[here - other + R, other] == 1
                rows_of[slot, 0:1, :] = jnp.where(listed, rows_of[slot, 0:1, :], UNLISTED)

                @pl.when(jnp.logical_not(jnp.logical_and(slot == 1, passing)))
                def _():
                    for piece in range(PARTS):
                        drain(qg.at[slot, :, pl.ds(piece * chunk, chunk), :], far_recv.at[slot, piece])

            item(index, slot)

            @pl.when(index == PARTS - 1)
            def _():
                there = far_slot(slot)
                for piece in range(PARTS):
                    lanes_of = slice(piece * chunk, (piece + 1) * chunk)
                    term_out[slot, piece] = acc_query[slot, :, lanes_of].astype(jnp.bfloat16)
                    remote(
                        term_out.at[slot, piece], term_in.at[there, piece],
                        term_send.at[slot], term_recv.at[there, piece], seq=other,
                    ).start()

    def send_rows(src, dst, which, place):
        to = sender(place)
        remote(src.at[part(place), :], dst.at[:, cols(head)], res_send.at[which], res_recv.at[which], head=to).start()

    def send_own(src, dst, which):
        pltpu.make_async_copy(src.at[part(0), :], dst.at[:, cols(head)], res_recv.at[which]).start()

    def finish(index):
        at = quarter(index)
        res_kv[0, at, :] = acc_key[at, :].astype(jnp.bfloat16)
        res_kv[1, at, :] = (acc_value[at, :] * (1.0 / SCALE)).astype(jnp.bfloat16)

        def step(place, carry):
            @pl.when(place > 0)
            def _():
                send_rows(res_kv.at[0], out_key, 1, place)
                send_rows(res_kv.at[1], out_value, 2, place)

            return carry

        lax.fori_loop(index * per, index * per + per, step, 0)

    def first_pass(index, carry):
        arrive(index)
        item(index, OWN)

        def step(turn, carry):
            far_item(index, ordered(turn))
            return carry

        return lax.fori_loop(0, NEAR, step, carry)

    def second_pass(index, carry):
        def step(turn, carry):
            far_item(index, ordered(turn))
            return carry

        lax.fori_loop(NEAR, SLOTS, step, 0)
        finish(index)
        return carry

    lax.fori_loop(0, PARTS, first_pass, 0)

    @pl.when(behind)
    def _():
        lax.fori_loop(0, PARTS, pass_on, 0)

    lax.fori_loop(0, PARTS, second_pass, 0)
    send_own(res_kv.at[0], out_key, 1)
    send_own(res_kv.at[1], out_value, 2)

    def query_part(index, carry):
        at = quarter(index)
        acc_part[...] = acc_query[OWN, :, at]
        for slot in range(SLOTS):

            @pl.when(neighbour(slot)[1])
            def _(slot=slot):
                drain(term_in.at[slot, index], term_recv.at[slot, index])
                acc_part[...] += term_in[slot, index].astype(jnp.float32)

        res_query[at, :] = acc_part[...].T.astype(jnp.bfloat16)

        def step(place, carry):
            @pl.when(place > 0)
            def _():
                send_rows(res_query, out_query, 0, place)

            return carry

        lax.fori_loop(index * per, index * per + per, step, 0)
        return carry

    lax.fori_loop(0, PARTS, query_part, 0)
    send_own(res_query, out_query, 0)

    sent = pl.ds(0, (nhead - 1) * rows)
    drain(qg.at[OWN, :, sent, :], qg_send)
    drain(kv.at[:, sent, :], kv_send)
    drain(delta_in.at[pl.ds(0, nhead - 1)], delta_send)
    for slot in range(SLOTS):
        inside = neighbour(slot)[1]

        @pl.when(passing if slot == 2 else inside)
        def _(slot=slot):
            for piece in range(PARTS):
                drain(qg.at[OWN, :, pl.ds(piece * chunk, chunk), :], far_send.at[slot, piece])

        @pl.when(inside)
        def _(slot=slot):
            drain(rows_of.at[OWN], rows_send.at[slot])
            drain(term_out.at[slot], term_send.at[slot])

    for which in range(3):
        drain(res_query.at[sent, :], res_send.at[which])
    drain(out_key, res_recv.at[1])
    drain(out_value, res_recv.at[2])
    drain(out_query, res_recv.at[0])


def per_device(query, key, value, attn_out, grad_out, lse, band):
    nseq, nhead = lax.axis_size("seq"), lax.axis_size("head")
    rows, width = query.shape
    block = rows * nhead
    low, full = jnp.bfloat16, jnp.float32
    vmem = pl.BlockSpec(memory_space=pltpu.VMEM)
    hbm = pl.BlockSpec(memory_space=pltpu.HBM)
    result = jax.ShapeDtypeStruct((rows, width), low)
    dma = pltpu.SemaphoreType.DMA

    def body(*refs):
        kernel(nseq, nhead, *refs)

    return pl.pallas_call(
        body,
        out_shape=(result,) * 3,
        in_specs=[hbm] * 6 + [pl.BlockSpec(memory_space=pltpu.SMEM)],
        out_specs=[vmem] * 3,
        scratch_shapes=[pltpu.VMEM((rows, width), low)] * 5
        + [
            pltpu.VMEM((1, block), full),
            pltpu.VMEM((block // HD, HD), full),
            pltpu.VMEM((HD, HD), full),
            pltpu.VMEM((SLOTS + 1, 2, block, HD), low),
            pltpu.VMEM((2, block, HD), low),
            pltpu.VMEM((SLOTS + 1, 2, block), full),
            pltpu.VMEM((nhead, 1, HD), full),
            pltpu.VMEM((nhead, 1, HD), full),
            pltpu.VMEM((PARTS, HD, block // PARTS), low),
            pltpu.VMEM((SLOTS + 1, HD, block), full),
            pltpu.VMEM((HD, block // PARTS), full),
            pltpu.VMEM((block, HD), full),
            pltpu.VMEM((block, HD), full),
            pltpu.VMEM((SLOTS, PARTS, HD, block // PARTS), low),
            pltpu.VMEM((SLOTS, PARTS, HD, block // PARTS), low),
            pltpu.VMEM((block, HD), low),
            pltpu.VMEM((2, block, HD), low),
            dma((6,)),
            dma, dma((PARTS,)), dma, dma((PARTS,)), dma, dma,
            dma((SLOTS, PARTS)), dma((SLOTS, PARTS)),
            dma((SLOTS,)), dma((SLOTS,)),
            dma((SLOTS,)), dma((SLOTS, PARTS)),
            dma((3,)), dma((3,)),
            pltpu.SemaphoreType.REGULAR((SLOTS,)),
        ],
        compiler_params=pltpu.CompilerParams(
            collective_id=0, has_side_effects=True, vmem_limit_bytes=62 * 2**20
        ),
        cost_estimate=pl.CostEstimate(
            flops=25 * 2 * block * block * HD, bytes_accessed=8 * rows * width * 2,
            transcendentals=5 * block * block,
        ),
        name="attention_grads",
    )(query, key, value, attn_out, grad_out, lse, band.T)


def solution(mesh):
    rows = P(("seq", "head"), None)
    return jax.shard_map(
        per_device, mesh=mesh, in_specs=(rows,) * 5 + (P("head", "seq"), P()),
        out_specs=(rows,) * 3, check_vma=False,
    )
```

time: 85.9 us -> 75.6 us (0.88)
  the two profiles are of different devices: /device:TPU:20 before, /device:TPU:5 now
where the time goes in v2:
time: 75.6 us; the launch traced here: 75.4 us
  Pallas kernels  71.3 us (94%)
  local copies, waits for them, and re-layouts  3.46 us (5%)
    pallas_call x1, Pallas kernels, per_device(): pl.pallas_call(body, out_shape=(result,) * 3, in_specs=[hbm] * 6 + [pl.Bl...  71.3 us
    unnamed x7, local copies, waits for them, and re-layouts  3.46 us

profile of v2, /device:TPU:5, one launch (start us, length us, event | category | flops | bytes accessed | tf_op | source)
XLA Modules:
  0.0 75.4 jit_solution(10808578238880696396)
XLA Ops:
  0.6 71.3 %attention_grads.1 = (bf16[64,2048]{1,0:T(8,128)(2,1)}, bf16[64,2048]{1,0:T(8,128)(2,1)}, bf16[64,2048]{1,0:T(8,128)(2,1)}) custom-call(bf16[64,2048]{1,0:T(8,128)(2,1)} %refs_0_.1, bf16[64,2048]{1,0:T(8,128)(2,1)} %refs_1_.1, bf16[64,2048]{1,0:T(8,128)(2,1)} %refs_2_.1, bf16[64,2048]{1,0:T(8,128)(2,1)} %refs_3_.1, bf16[64,2048]{1,0:T(8,128)(2,1)} %refs_4_.1, ...), custom_call_target="tpu_custom_call" | custom-call | flops 6710886400 | bytes 2097152 | tf_op jit(solution)/shard_map/attention_grads/pallas_call | solution.py:499
  71.9 0.0 copy-start.1
  71.9 1.7 %copy.13 = bf16[64,2048]{1,0:T(8,128)(2,1)} copy(bf16[64,2048]{1,0:T(8,128)(2,1)} %get-tuple-element.6) | data formatting | bytes 524288
  73.6 0.0 copy-done.1
  73.6 0.0 copy-start
  73.6 0.7 copy.14
  74.3 0.3 copy-done
  74.7 0.7 copy.15
Async XLA Ops:
  71.9 1.7 %copy-start.1 = (bf16[64,2048]{1,0:T(8,128)(2,1)S(1)}, bf16[64,2048]{1,0:T(8,128)(2,1)}, u32[]{:S(2)}) copy-start(bf16[64,2048]{1,0:T(8,128)(2,1)} %get-tuple-element.7) | copy-start | bytes 786436
  73.6 1.0 %copy-start = (bf16[64,2048]{1,0:T(8,128)(2,1)S(1)}, bf16[64,2048]{1,0:T(8,128)(2,1)}, u32[]{:S(2)}) copy-start(bf16[64,2048]{1,0:T(8,128)(2,1)} %get-tuple-element.8) | copy-start | bytes 786436

commit v3 on v2

--- a/solution.py
+++ b/solution.py
@@ -14,7 +14,6 @@
 PARTS = 4
 FIRST = 4
 AFTER = ((1, (4,)), (2, (5,)), (3, (6,)))
-NEAR = 1
 LOG2E = 1.4426950408889634
 SCALE = 1.0 / math.sqrt(HD)
 UNLISTED = 1e30
@@ -92,6 +91,8 @@
     sign = 1 - 2 * lax.rem(here, 2)
     row = nseq // 2 if nseq >= 8 * R else nseq
     place_in_row = lax.rem(here, row)
+    at_end = jnp.logical_or(place_in_row == 0, place_in_row == row - 1)
+    beside_end = jnp.logical_or(place_in_row == 1, place_in_row == row - 2)
     rows = query.shape[0]
     block = rows * nhead
     chunk = block // PARTS
@@ -140,10 +141,13 @@
         return other, later, earlier, jnp.logical_and(inside, ahead > R)
 
     def ordered(turn):
-        last = jnp.where(turn < 3, lax.rem(turn + 1, 3), turn)
-        slot = jnp.where(place_in_row == 0, lax.rem(SLOTS - turn, SLOTS), turn)
-        slot = jnp.where(place_in_row == row - 1, last, slot)
-        return jnp.where(place_in_row == row - 2, lax.rem(turn + 3, SLOTS), slot)
+        early_last = jnp.where(turn == 1, 3, jnp.where(turn > 1, turn - 1, 0))
+        late_first = jnp.where(turn > 1, 5 - turn, turn)
+        slot = jnp.where(place_in_row == 0, early_last, turn)
+        return jnp.where(place_in_row >= row - 2, late_first, slot)
+
+    near = jnp.where(at_end, 1, 2)
+    whole = jnp.where(jnp.logical_or(at_end, beside_end), 1, 0)
 
     def remote(src, dst, send, recv, **where):
         return pltpu.make_async_remote_copy(
@@ -297,7 +301,6 @@
     lax.fori_loop(0, PARTS, forward, 0)
 
     passing = neighbour(1)[1]
-    behind = jnp.logical_and(passing, place_in_row == 0)
 
     def pass_on(index, carry):
         at = quarter(index)
@@ -325,10 +328,6 @@
         def _(slot=slot, other=other):
             there = slot if slot < 2 else 5 - slot
             remote(rows_of.at[OWN], rows_of.at[there], rows_send.at[slot], rows_recv.at[there], seq=other).start()
-
-    @pl.when(jnp.logical_and(passing, jnp.logical_not(behind)))
-    def _():
-        lax.fori_loop(0, PARTS, pass_on, 0)
 
     def arrive(index):
         at = quarter(index)
@@ -365,7 +364,11 @@
                 listed = band[here - other + R, other] == 1
                 rows_of[slot, 0:1, :] = jnp.where(listed, rows_of[slot, 0:1, :], UNLISTED)
 
-                @pl.when(jnp.logical_not(jnp.logical_and(slot == 1, passing)))
+                @pl.when(slot == 1)
+                def _():
+                    lax.fori_loop(0, PARTS, pass_on, 0)
+
+                @pl.when(slot != 1)
                 def _():
                     for piece in range(PARTS):
                         drain(qg.at[slot, :, pl.ds(piece * chunk, chunk), :], far_recv.at[slot, piece])
@@ -413,23 +416,26 @@
             far_item(index, ordered(turn))
             return carry
 
-        return lax.fori_loop(0, NEAR, step, carry)
+        return lax.fori_loop(0, near, step, carry)
+
+    def whole_pass(turn, carry):
+        def step(index, carry):
+            far_item(index, ordered(turn))
+            return carry
+
+        return lax.fori_loop(0, PARTS, step, carry)
 
     def second_pass(index, carry):
         def step(turn, carry):
             far_item(index, ordered(turn))
             return carry
 
-        lax.fori_loop(NEAR, SLOTS, step, 0)
+        lax.fori_loop(near + whole, SLOTS, step, 0)
         finish(index)
         return carry
 
     lax.fori_loop(0, PARTS, first_pass, 0)
-
-    @pl.when(behind)
-    def _():
-        lax.fori_loop(0, PARTS, pass_on, 0)
-
+    lax.fori_loop(near, near + whole, whole_pass, 0)
     lax.fori_loop(0, PARTS, second_pass, 0)
     send_own(res_kv.at[0], out_key, 1)
     send_own(res_kv.at[1], out_value, 2)
@@ -500,7 +506,7 @@
         body,
         out_shape=(result,) * 3,
         in_specs=[hbm] * 6 + [pl.BlockSpec(memory_space=pltpu.SMEM)],
-        out_specs=[vmem] * 3,
+        out_specs=[hbm] * 3,
         scratch_shapes=[pltpu.VMEM((rows, width), low)] * 5
         + [
             pltpu.VMEM((1, block), full),

time: 75.6 us -> 73.6 us (0.974)
  Pallas kernels: 71.3 us -> 69.2 us
    pallas_call x1, Pallas kernels: 71.3 us -> 69.2 us  [per_device(): pl.pallas_call(body, out_shape=(result,) * 3, in_specs=[hbm] * 6 + [pl.Bl...]
where the time goes in v3:
time: 73.6 us; the launch traced here: 73.4 us
  Pallas kernels  69.2 us (94%)
  local copies, waits for them, and re-layouts  3.46 us (5%)
    pallas_call x1, Pallas kernels, per_device(): pl.pallas_call(body, out_shape=(result,) * 3, in_specs=[hbm] * 6 + [pl.Bl...  69.2 us
    unnamed x7, local copies, waits for them, and re-layouts  3.46 us

profile of v3, /device:TPU:5, one launch (start us, length us, event | category | flops | bytes accessed | tf_op | source)
XLA Modules:
  0.0 73.4 jit_solution(1586641135171044206)
XLA Ops:
  0.6 69.2 %attention_grads.1 = (bf16[64,2048]{1,0:T(8,128)(2,1)}, bf16[64,2048]{1,0:T(8,128)(2,1)}, bf16[64,2048]{1,0:T(8,128)(2,1)}) custom-call(bf16[64,2048]{1,0:T(8,128)(2,1)} %refs_0_.1, bf16[64,2048]{1,0:T(8,128)(2,1)} %refs_1_.1, bf16[64,2048]{1,0:T(8,128)(2,1)} %refs_2_.1, bf16[64,2048]{1,0:T(8,128)(2,1)} %refs_3_.1, bf16[64,2048]{1,0:T(8,128)(2,1)} %refs_4_.1, ...), custom_call_target="tpu_custom_call" | custom-call | flops 6710886400 | bytes 2097152 | tf_op jit(solution)/shard_map/attention_grads/pallas_call | solution.py:505
  69.9 0.0 copy-start.1
  69.9 1.7 %copy.13 = bf16[64,2048]{1,0:T(8,128)(2,1)} copy(bf16[64,2048]{1,0:T(8,128)(2,1)} %get-tuple-element.6) | data formatting | bytes 524288
  71.6 0.0 copy-done.1
  71.6 0.0 copy-start
  71.6 0.7 copy.14
  72.3 0.3 copy-done
  72.7 0.7 copy.15
Async XLA Ops:
  69.9 1.7 %copy-start.1 = (bf16[64,2048]{1,0:T(8,128)(2,1)S(1)}, bf16[64,2048]{1,0:T(8,128)(2,1)}, u32[]{:S(2)}) copy-start(bf16[64,2048]{1,0:T(8,128)(2,1)} %get-tuple-element.7) | copy-start | bytes 786436
  71.6 1.0 %copy-start = (bf16[64,2048]{1,0:T(8,128)(2,1)S(1)}, bf16[64,2048]{1,0:T(8,128)(2,1)}, u32[]{:S(2)}) copy-start(bf16[64,2048]{1,0:T(8,128)(2,1)} %get-tuple-element.8) | copy-start | bytes 786436

commit v4 on v3

--- a/solution.py
+++ b/solution.py
@@ -496,7 +496,6 @@
     low, full = jnp.bfloat16, jnp.float32
     vmem = pl.BlockSpec(memory_space=pltpu.VMEM)
     hbm = pl.BlockSpec(memory_space=pltpu.HBM)
-    result = jax.ShapeDtypeStruct((rows, width), low)
     dma = pltpu.SemaphoreType.DMA
 
     def body(*refs):
@@ -504,9 +503,9 @@
 
     return pl.pallas_call(
         body,
-        out_shape=(result,) * 3,
+        out_shape=(pltpu.VMEM((rows, width), low),) * 3,
         in_specs=[hbm] * 6 + [pl.BlockSpec(memory_space=pltpu.SMEM)],
-        out_specs=[hbm] * 3,
+        out_specs=[vmem] * 3,
         scratch_shapes=[pltpu.VMEM((rows, width), low)] * 5
         + [
             pltpu.VMEM((1, block), full),

time: 73.6 us -> 72 us (0.978)
  local copies, waits for them, and re-layouts: 3.46 us -> 2.11 us
    unnamed x7 -> x3, local copies, waits for them, and re-layouts: 3.46 us -> 2.11 us
where the time goes in v4:
time: 72 us; the launch traced here: 71.9 us
  Pallas kernels  69.1 us (96%)
  local copies, waits for them, and re-layouts  2.11 us (3%)
    pallas_call x1, Pallas kernels, per_device(): pl.pallas_call(body, out_shape=(pltpu.VMEM((rows, width), low),) * 3, in_...  69.1 us
    unnamed x3, local copies, waits for them, and re-layouts  2.11 us

profile of v4, /device:TPU:5, one launch (start us, length us, event | category | flops | bytes accessed | tf_op | source)
XLA Modules:
  0.0 71.9 jit_solution(6121499832876729728)
XLA Ops:
  0.6 69.1 %attention_grads.1 = (bf16[64,2048]{1,0:T(8,128)(2,1)S(1)}, bf16[64,2048]{1,0:T(8,128)(2,1)S(1)}, bf16[64,2048]{1,0:T(8,128)(2,1)S(1)}) custom-call(bf16[64,2048]{1,0:T(8,128)(2,1)} %refs_0_.1, bf16[64,2048]{1,0:T(8,128)(2,1)} %refs_1_.1, bf16[64,2048]{1,0:T(8,128)(2,1)} %refs_2_.1, bf16[64,2048]{1,0:T(8,128)(2,1)} %refs_3_.1, bf16[64,2048]{1,0:T(8,128)(2,1)} %refs_4_.1, ...), custom_call_target="tpu_custom_call" | custom-call | flops 6710886400 | bytes 2097152 | tf_op jit(solution)/shard_map/attention_grads/pallas_call | solution.py:504
  69.8 0.7 copy.13
  70.5 0.7 copy.14
  71.2 0.7 copy.15

commit v5 on v4

--- a/solution.py
+++ b/solution.py
@@ -144,7 +144,7 @@
         early_last = jnp.where(turn == 1, 3, jnp.where(turn > 1, turn - 1, 0))
         late_first = jnp.where(turn > 1, 5 - turn, turn)
         slot = jnp.where(place_in_row == 0, early_last, turn)
-        return jnp.where(place_in_row >= row - 2, late_first, slot)
+        return jnp.where(place_in_row == row - 2, late_first, slot)
 
     near = jnp.where(at_end, 1, 2)
     whole = jnp.where(jnp.logical_or(at_end, beside_end), 1, 0)

time: 72 us -> 71.8 us (level)
  no operation moved by 1% of the time
where the time goes in v5:
time: 71.8 us; the launch traced here: 71.6 us
  Pallas kernels  68.9 us (96%)
  local copies, waits for them, and re-layouts  2.11 us (3%)
    pallas_call x1, Pallas kernels, per_device(): pl.pallas_call(body, out_shape=(pltpu.VMEM((rows, width), low),) * 3, in_...  68.9 us
    unnamed x3, local copies, waits for them, and re-layouts  2.11 us

profile of v5, /device:TPU:5, one launch (start us, length us, event | category | flops | bytes accessed | tf_op | source)
XLA Modules:
  0.0 71.6 jit_solution(7177487891388632516)
XLA Ops:
  0.6 68.9 %attention_grads.1 = (bf16[64,2048]{1,0:T(8,128)(2,1)S(1)}, bf16[64,2048]{1,0:T(8,128)(2,1)S(1)}, bf16[64,2048]{1,0:T(8,128)(2,1)S(1)}) custom-call(bf16[64,2048]{1,0:T(8,128)(2,1)} %refs_0_.1, bf16[64,2048]{1,0:T(8,128)(2,1)} %refs_1_.1, bf16[64,2048]{1,0:T(8,128)(2,1)} %refs_2_.1, bf16[64,2048]{1,0:T(8,128)(2,1)} %refs_3_.1, bf16[64,2048]{1,0:T(8,128)(2,1)} %refs_4_.1, ...), custom_call_target="tpu_custom_call" | custom-call | flops 6710886400 | bytes 2097152 | tf_op jit(solution)/shard_map/attention_grads/pallas_call | solution.py:504
  69.5 0.7 copy.13
  70.2 0.7 copy.14
  70.9 0.7 copy.15
